TPU v7x, 1024 devices: a whole 4x8x16 slice. The times are simulated.
1024 devices in a mesh: dp: 16 (over y, core), expert: 64 (over z, x).
Axes of the slice: x: 4, y: 8, z: 16, core: 2. Of those that a mesh axis runs over, the one named last changes fastest.
Arguments:
- tokens: bfloat16 [131072, 4096], P(('dp', 'expert')), may hold values from -24 to 24
- cotangent: bfloat16 [131072, 4096], P(('dp', 'expert')), may hold values from -24 to 24
- slot_token: int32 [1024, 16], P(('dp', 'expert')), may hold values from 0 to 127, as said below
- slot_gate: int32 [1024, 16], P(('dp', 'expert')), may hold values from 0 to 1023, as said below
- gate_weight: bfloat16 [4096, 8192], P(None, 'expert'), may hold values from -0.09375 to 0.09375
- up_weight: bfloat16 [4096, 8192], P(None, 'expert'), may hold values from -0.09375 to 0.09375
- down_weight: bfloat16 [8192, 4096], P('expert'), may hold values from -0.1875 to 0.1875
Outputs:
- token_grad: bfloat16 [131072, 4096], P(('dp', 'expert'))
- gate_grad: bfloat16 [4096, 8192], P('dp', 'expert')
- up_grad: bfloat16 [4096, 8192], P('dp', 'expert')
- down_grad: bfloat16 [8192, 4096], P('expert', 'dp')
Inputs may be any that keep to these rules, and one draw needn't show every extreme that they name: `slot_token`: entry f * 2 + k of row r is the token within block r in the k-th slot that expert f fills from that block; the 2 entries of one block and expert are distinct. `slot_gate`: the gate weight is the code / 1024; a code is 0 exactly in an empty slot, and the empty slots of one block and expert follow its filled ones. Each block fills 0 to 2 slots of each expert; blocks 2i and 2i + 1 of a data group together fill exactly 2 slots of each expert; some block of every data group fills all 2 of each expert, and each expert fills exactly 64 slots over the 64 blocks of one data group.
All inputs are finite; a program needn't handle non-finite values.
Results may differ from a plain program's by a relative error of at most 0.023.
Values may be sent and summed in bfloat16 or wider, within the bound.
A program may use at most 32 MiB of HBM per device.

v0:
```python
import jax
import jax.numpy as jnp
from jax import lax
from jax.sharding import PartitionSpec as P

FF = 1024


def shards(tokens, cotangent, slot_token, slot_gate, gate_weight, up_weight, down_weight):
    model_width = tokens.shape[1]
    block_tokens = tokens.shape[0]
    hidden_width = gate_weight.shape[1]
    shard_count = FF // hidden_width
    flight = lax.axis_size("expert") // shard_count
    slot_count = slot_token.shape[1] // flight
    first_axes = (((0,), (0,)), ((), ()))
    second_axes = (((1,), (1,)), ((), ()))
    chosen = slot_token[0]
    weights = slot_gate[0].astype(jnp.float32) / 1024.0
    token_rows = jnp.take(tokens, chosen, axis=0)
    gated_rows = (
        weights[:, None] * jnp.take(cotangent, chosen, axis=0).astype(jnp.float32)
    ).astype(jnp.bfloat16)
    own_rows = token_rows.reshape(flight, slot_count, model_width)
    own_grads = gated_rows.reshape(flight, slot_count, model_width)

    def spread(rows):
        per_slot = rows.shape[1]
        widened = jnp.broadcast_to(
            rows.reshape(flight, 1, per_slot, model_width),
            (flight, shard_count, per_slot, model_width),
        )
        return widened.reshape(flight * shard_count, per_slot, model_width)

    moved_rows, moved_grads = (
        lax.all_to_all(spread(own_rows), "expert", split_axis=0, concat_axis=0, tiled=True),
        lax.all_to_all(spread(own_grads), "expert", split_axis=0, concat_axis=0, tiled=True),
    )
    per_slot = moved_rows.shape[1]
    row_count = moved_rows.shape[0] * per_slot
    taken_rows = moved_rows.reshape(row_count, model_width)
    taken_grads = moved_grads.reshape(row_count, model_width)
    pre_gate = jnp.dot(taken_rows, gate_weight, preferred_element_type=jnp.float32)
    pre_up = jnp.dot(taken_rows, up_weight, preferred_element_type=jnp.float32)
    sigmoid_gate = jax.nn.sigmoid(pre_gate)
    activated = pre_gate * sigmoid_gate
    hidden_act = (activated * pre_up).astype(jnp.bfloat16)
    hidden_grad = lax.dot_general(
        taken_grads, down_weight, second_axes, preferred_element_type=jnp.float32
    )
    grad_gate = (
        hidden_grad * pre_up * sigmoid_gate * (1.0 + pre_gate * (1.0 - sigmoid_gate))
    ).astype(jnp.bfloat16)
    grad_up = (hidden_grad * activated).astype(jnp.bfloat16)
    partials = lax.dot_general(
        grad_gate, gate_weight, second_axes, preferred_element_type=jnp.float32
    )
    partials = (
        partials
        + lax.dot_general(grad_up, up_weight, second_axes, preferred_element_type=jnp.float32)
    ).astype(jnp.bfloat16)
    returned = lax.all_to_all(
        partials.reshape(flight * shard_count, per_slot, model_width),
        "expert",
        split_axis=0,
        concat_axis=0,
        tiled=True,
    )
    target = jnp.broadcast_to(
        chosen.reshape(flight, 1, slot_count), (flight, shard_count, slot_count)
    ).reshape(row_count)
    one_hot = (jnp.arange(block_tokens, dtype=jnp.int32)[:, None] == target[None, :]).astype(
        jnp.bfloat16
    )
    summed = jnp.dot(
        one_hot, returned.reshape(row_count, model_width), preferred_element_type=jnp.float32
    )
    token_grad = summed.astype(jnp.bfloat16)
    gate_part = lax.dot_general(
        taken_rows, grad_gate, first_axes, preferred_element_type=jnp.float32
    )
    up_part = lax.dot_general(taken_rows, grad_up, first_axes, preferred_element_type=jnp.float32)
    down_part = lax.dot_general(
        hidden_act, taken_grads, first_axes, preferred_element_type=jnp.float32
    )
    gate_sum, up_sum, down_sum = (
        lax.psum_scatter(
            gate_part.astype(jnp.bfloat16), "dp", scatter_dimension=0, tiled=True
        ).astype(jnp.float32),
        lax.psum_scatter(
            up_part.astype(jnp.bfloat16), "dp", scatter_dimension=0, tiled=True
        ).astype(jnp.float32),
        lax.psum_scatter(
            down_part.astype(jnp.bfloat16), "dp", scatter_dimension=1, tiled=True
        ).astype(jnp.float32),
    )
    return (
        token_grad,
        gate_sum.astype(jnp.bfloat16),
        up_sum.astype(jnp.bfloat16),
        down_sum.astype(jnp.bfloat16),
    )


def solution(mesh):
    placed = (
        P(("dp", "expert"), None),
        P(("dp", "expert"), None),
        P(("dp", "expert"), None),
        P(("dp", "expert"), None),
        P(None, "expert"),
        P(None, "expert"),
        P("expert", None),
    )
    return jax.shard_map(
        shards,
        mesh=mesh,
        in_specs=placed,
        out_specs=(
            P(("dp", "expert"), None),
            P("dp", "expert"),
            P("dp", "expert"),
            P("expert", "dp"),
        ),
        check_vma=False,
    )
```

profile of v0, /device:TPU:1, one launch (start us, length us, event | category | flops | bytes accessed | tf_op | source)
XLA Modules:
  0.0 357.7 jit_solution(4087607996719316362)
XLA Ops:
  7.2 0.0 copy-start
  7.2 0.8 compare_and_fusion
  7.9 0.7 compare_select_fusion
  8.6 2.1 gather_fusion.1
  10.7 0.0 copy-start.3
  10.7 0.1 broadcast_select_fusion
  10.8 0.1 broadcast_in_dim.36
  10.9 0.0 copy-start.4
  10.9 2.0 broadcast_in_dim.37
  12.9 22.8 %all-to-all-start.1 = ((bf16[64,2,4096]{2,1,0:T(2,128)(2,1)}), bf16[64,2,4096]{2,1,0:T(2,128)(2,1)S(1)}, u32[]{:S(2)}, u32[]{:S(2)}) async-start(bf16[64,2,4096]{2,1,0:T(2,128)(2,1)} %bitcast.3), calls=%async_computation.1 | async-start | bytes 2097152 | tf_op jit(solution)/shard_map/all_to_all | solution.py:36
  35.7 0.6 gather_fusion
  36.4 0.1 multiply_convert_fusion
  36.5 0.1 broadcast_in_dim.34
  36.6 50.6 %all-to-all-done.1 = bf16[64,2,4096]{2,1,0:T(2,128)(2,1)S(1)} async-done(((bf16[64,2,4096]{2,1,0:T(2,128)(2,1)}), bf16[64,2,4096]{2,1,0:T(2,128)(2,1)S(1)}, u32[]{:S(2)}, u32[]{:S(2)}) %all-to-all-start.1) | async-done | bytes 1048608 | tf_op jit(solution)/shard_map/all_to_all | solution.py:36
  87.1 2.0 broadcast_in_dim.35
  89.1 9.3 %all-to-all-start = ((bf16[64,2,4096]{2,1,0:T(2,128)(2,1)}), bf16[64,2,4096]{2,1,0:T(2,128)(2,1)}, u32[]{:S(2)}, u32[]{:S(2)}) async-start(bf16[64,2,4096]{2,1,0:T(2,128)(2,1)} %bitcast.2), calls=%async_computation | async-start | bytes 2097152 | tf_op jit(solution)/shard_map/all_to_all | solution.py:37
  98.4 0.0 reduce-scatter.8.cloned.1.call-start
  98.5 0.4 reshape.47
  98.9 0.0 copy-start.1
  98.9 0.4 fusion.6
  99.4 0.8 copy-done.1
  100.2 0.4 fusion.5
  100.6 48.7 %all-to-all-done = bf16[64,2,4096]{2,1,0:T(2,128)(2,1)} async-done(((bf16[64,2,4096]{2,1,0:T(2,128)(2,1)}), bf16[64,2,4096]{2,1,0:T(2,128)(2,1)}, u32[]{:S(2)}, u32[]{:S(2)}) %all-to-all-start) | async-done | bytes 1048608 | tf_op jit(solution)/shard_map/all_to_all | solution.py:37
  149.3 1.5 reshape.45
  150.7 1.5 convolution_convert_fusion
  152.2 0.0 reduce-scatter.8.cloned.1.call-update
  152.2 1.7 multiply_convert_fusion.2
  153.9 0.0 copy-start.2
  153.9 0.4 fusion.7
  154.3 0.8 copy-done.2
  155.1 0.4 fusion
  155.6 1.5 reshape.48
  157.1 8.6 %all-to-all-start.2 = ((bf16[64,2,4096]{2,1,0:T(2,128)(2,1)}), bf16[64,2,4096]{2,1,0:T(2,128)(2,1)S(1)}, u32[]{:S(2)}, u32[]{:S(2)}) async-start(bf16[64,2,4096]{2,1,0:T(2,128)(2,1)} %reshape.48), calls=%async_computation.2 | async-start | bytes 2097152 | tf_op jit(solution)/shard_map/all_to_all | solution.py:62
  165.6 0.0 reduce-scatter.4.cloned.1.call-start
  165.7 1.5 convolution_convert_fusion.2
  167.1 0.0 reduce-scatter.4.cloned.1.call-update
  167.2 0.0 reduce-scatter.6.cloned.1.call-start
  167.2 1.5 convolution_convert_fusion.1
  168.7 0.0 reduce-scatter.6.cloned.1.call-update
  168.7 0.5 broadcast.62
  169.3 0.6 reduce.3
  169.8 0.1 broadcast_in_dim.32
  169.9 0.1 eq.16
  170.1 45.0 %all-to-all-done.2 = bf16[64,2,4096]{2,1,0:T(2,128)(2,1)S(1)} async-done(((bf16[64,2,4096]{2,1,0:T(2,128)(2,1)}), bf16[64,2,4096]{2,1,0:T(2,128)(2,1)S(1)}, u32[]{:S(2)}, u32[]{:S(2)}) %all-to-all-start.2) | async-done | bytes 1048608 | tf_op jit(solution)/shard_map/all_to_all | solution.py:62
  215.1 0.4 reshape.49
  215.5 1.4 convolution_convert_fusion.3
  216.9 66.2 %reduce-scatter.4.cloned.1.call-done = bf16[256,128]{1,0:T(8,128)(2,1)} async-done(((bf16[4096,128]{1,0:T(8,128)(2,1)}), bf16[256,128]{1,0:T(8,128)(2,1)}) %reduce-scatter.4.cloned.1.call-update) | async-done | bytes 65552 | tf_op jit(solution)/shard_map/reduce_scatter | solution.py:87
  283.1 68.1 %reduce-scatter.6.cloned.1.call-done = bf16[256,128]{1,0:T(8,128)(2,1)} async-done(((bf16[4096,128]{1,0:T(8,128)(2,1)}), bf16[256,128]{1,0:T(8,128)(2,1)}) %reduce-scatter.6.cloned.1.call-update) | async-done | bytes 65552 | tf_op jit(solution)/shard_map/reduce_scatter | solution.py:90
  (9 shorter events, 0.0 us)
Async XLA Ops:
  7.2 91.8 %copy-start = (bf16[4096,128]{1,0:T(8,128)(2,1)S(1)}, bf16[4096,128]{1,0:T(8,128)(2,1)}, u32[]{:S(2)}) copy-start(bf16[4096,128]{1,0:T(8,128)(2,1)} %param.13) | copy-start | bytes 3145732
  10.7 25.0 %copy-start.3 = (bf16[128,4096]{1,0:T(8,128)(2,1)S(1)}, bf16[128,4096]{1,0:T(8,128)(2,1)}, u32[]{:S(2)}) copy-start(bf16[128,4096]{1,0:T(8,128)(2,1)} %param.10) | copy-start | bytes 3145732
  10.9 25.4 %copy-start.4 = (s32[1,16]{1,0:T(1,128)S(1)}, s32[1,16]{1,0:T(1,128)}, u32[]{:S(2)}) copy-start(s32[1,16]{1,0:T(1,128)} %param.12) | copy-start | bytes 196
  12.9 74.2 %all-to-all-start.1 = ((bf16[64,2,4096]{2,1,0:T(2,128)(2,1)}), bf16[64,2,4096]{2,1,0:T(2,128)(2,1)S(1)}, u32[]{:S(2)}, u32[]{:S(2)}) async-start(bf16[64,2,4096]{2,1,0:T(2,128)(2,1)} %bitcast.3), calls=%async_computation.1 | async-start | bytes 2097152 | tf_op jit(solution)/shard_map/all_to_all | solution.py:36
  89.1 60.1 %all-to-all-start = ((bf16[64,2,4096]{2,1,0:T(2,128)(2,1)}), bf16[64,2,4096]{2,1,0:T(2,128)(2,1)}, u32[]{:S(2)}, u32[]{:S(2)}) async-start(bf16[64,2,4096]{2,1,0:T(2,128)(2,1)} %bitcast.2), calls=%async_computation | async-start | bytes 2097152 | tf_op jit(solution)/shard_map/all_to_all | solution.py:37
  98.4 118.5 %reduce-scatter.8.cloned.1.call-start = ((), (), s32[]{:S(2)}) async-start(), calls=%async_computation.8 | async-start | bytes 1114112 | tf_op jit(solution)/shard_map/reduce_scatter | solution.py:93
  98.9 1.2 copy-start.1
  153.9 1.2 copy-start.2
  157.1 58.0 %all-to-all-start.2 = ((bf16[64,2,4096]{2,1,0:T(2,128)(2,1)}), bf16[64,2,4096]{2,1,0:T(2,128)(2,1)S(1)}, u32[]{:S(2)}, u32[]{:S(2)}) async-start(bf16[64,2,4096]{2,1,0:T(2,128)(2,1)} %reshape.48), calls=%async_computation.2 | async-start | bytes 2097152 | tf_op jit(solution)/shard_map/all_to_all | solution.py:62
  165.6 117.4 %reduce-scatter.4.cloned.1.call-start = ((), (), s32[]{:S(2)}) async-start(), calls=%async_computation.6 | async-start | bytes 1114112 | tf_op jit(solution)/shard_map/reduce_scatter | solution.py:87
  167.1 2.1 copy-start.5
  167.2 184.0 %reduce-scatter.6.cloned.1.call-start = ((), (), s32[]{:S(2)}) async-start(), calls=%async_computation.7 | async-start | bytes 1114112 | tf_op jit(solution)/shard_map/reduce_scatter | solution.py:90
Sparse Core Ops, SparseCore 0:
  152.3 61.7 reduce-scatter.7
  218.5 64.5 reduce-scatter.3
  287.0 64.1 reduce-scatter.5
where the time goes:
time: 358 us
  waiting for transfers between devices  279 us (78%)
  starting transfers between devices  40.8 us (11%)
  between operations  13.9 us (4%)
  local copies, waits for them, and re-layouts  13.1 us (4%)
  matrix products  9.23 us (3%)
    reduce_scatter x1, waiting for transfers between devices, shards(): lax.psum_scatter(up_part.astype(jnp.bfloat16), 'dp', scatter_dimension=0,...  68.1 us
    reduce_scatter x1, waiting for transfers between devices, shards(): lax.psum_scatter(gate_part.astype(jnp.bfloat16), 'dp', scatter_dimension=...  66.2 us
    all_to_all x1, waiting for transfers between devices, shards(): lax.all_to_all(spread(own_rows), 'expert', split_axis=0, concat_axis=0, t...  50.6 us
    all_to_all x1, waiting for transfers between devices, shards(): lax.all_to_all(spread(own_grads), 'expert', split_axis=0, concat_axis=0,...  48.7 us
    all_to_all x1, waiting for transfers between devices, shards(): lax.all_to_all(partials.reshape(flight * shard_count, per_slot, model_wid...  45 us
    all_to_all x1, starting transfers between devices, shards(): lax.all_to_all(spread(own_rows), 'expert', split_axis=0, concat_axis=0, t...  22.8 us
    all_to_all x1, starting transfers between devices, shards(): lax.all_to_all(spread(own_grads), 'expert', split_axis=0, concat_axis=0,...  9.29 us
    all_to_all x1, starting transfers between devices, shards(): lax.all_to_all(partials.reshape(flight * shard_count, per_slot, model_wid...  8.57 us
  transfers between devices with their start and end apart: 6, of which 5 were waited for; matrix products, arithmetic and copies ran while one was open for 3% of the time, Pallas kernels for 0%

commit v1 on v0

v1 whole, which is shorter than its diff:
```python
import jax
import jax.numpy as jnp
from jax import lax
from jax.experimental import pallas as pl
from jax.experimental.pallas import tpu as pltpu
from jax.sharding import PartitionSpec as P

F32 = jnp.float32
BF16 = jnp.bfloat16
MESH = pl.DeviceIdType.MESH

X = 4
Y = 8
Z = 16
D = 4096
HALF = D // 2
FLIGHT = 8
TOK = 128
HD = 128
BLOCK = 16
ROWS = BLOCK * X
SLICE = 256
GRADS = 3 * HD
PIECES = 4
PIECE = GRADS // PIECES
MID = HALF // 2


def lanes(a, b):
    return lax.dot_general(a, b, (((1,), (1,)), ((), ())), preferred_element_type=F32)


def dot(a, b):
    return jnp.dot(a, b, preferred_element_type=F32)


def kernel(
    st, sg, tok_hbm, cot_hbm, wg_hbm, wu_hbm, wd_hbm,
    tg_out, gg_out, ug_out, dg_out,
    tok, cot, w, wd, tile, tile2, merged, give, got, zin, rows, dab, gt,
    part, d2d, rout, rin, pz_out, pz_in, pm, pa_out, pa_in, pb_out, pb_in,
    zq_out, zq_in, pq_in, prow,
    load_sem, pair_s, pair_r, z_s, z_r, ag_s, ag_r, d2d_s, d2d_r, ring_s, ring_r,
    pz_sem, pa_s, pa_r, pb_s, pb_r, zq_sem, pq_sem,
):
    d = lax.axis_index("dp")
    e = lax.axis_index("expert")
    y, core = d // 2, d % 2
    z, x = e // X, e % X
    h = z % 2
    other_core = {"dp": y * 2 + 1 - core}
    y_next = {"dp": (y + 1) % Y * 2 + core}
    y_prev = {"dp": (y + Y - 1) % Y * 2 + core}
    x_next = {"expert": z * X + (x + 1) % X}
    x_prev = {"expert": z * X + (x + X - 1) % X}
    x_pair = {"expert": e + 1 - 2 * (x % 2)}
    z_pair = {"expert": e + X - 2 * X * h}

    def remote(src, dst, send_sem, recv_sem, to):
        return pltpu.make_async_remote_copy(
            src_ref=src, dst_ref=dst, send_sem=send_sem, recv_sem=recv_sem,
            device_id=to, device_id_type=MESH,
        )

    sent = []

    def send(src, dst, send_sem, recv_sem, to):
        copy = remote(src, dst, send_sem, recv_sem, to)
        copy.start()
        sent.append(copy)

    def arrived(dst, recv_sem):
        remote(dst, dst, recv_sem, recv_sem, other_core).wait_recv()

    barrier = pltpu.get_barrier_semaphore()

    def z_at(i):
        return (z + i) % Z

    def greet(i, carry):
        pl.semaphore_signal(
            barrier, inc=1, device_id={"expert": z_at(i) * X + x}, device_id_type=MESH
        )
        return carry

    for to in (x_next, x_prev, other_core, y_next, y_prev):
        pl.semaphore_signal(barrier, inc=1, device_id=to, device_id_type=MESH)
    lax.fori_loop(1, Z, greet, 0)

    loads = [
        pltpu.make_async_copy(src, dst, load_sem.at[i])
        for i, (src, dst) in enumerate(
            (
                (tok_hbm, tok),
                (cot_hbm, cot),
                (wg_hbm, w.at[:, 0:HD]),
                (wu_hbm, w.at[:, HD : 2 * HD]),
                (wd_hbm, wd),
            )
        )
    ]
    for copy in loads:
        copy.start()

    line = lax.broadcasted_iota(jnp.int32, (BLOCK, TOK), 0)
    lane = lax.broadcasted_iota(jnp.int32, (BLOCK, TOK), 1)
    row_t = lax.broadcasted_iota(jnp.int32, (TOK, BLOCK), 0)
    col_t = lax.broadcasted_iota(jnp.int32, (TOK, BLOCK), 1)
    pick = jnp.zeros((BLOCK, TOK), F32)
    pick_t = jnp.zeros((TOK, BLOCK), F32)
    weight = jnp.zeros((BLOCK, TOK), F32)
    for k in range(2):
        for f in range(FLIGHT):
            s = k * FLIGHT + f
            code = sg[0, f * 2 + k]
            token = jnp.where(code != 0, st[0, f * 2 + k], -1)
            pick = jnp.where((line == s) & (lane == token), 1.0, pick)
            pick_t = jnp.where((col_t == s) & (row_t == token), 1.0, pick_t)
            weight = jnp.where(line == s, code.astype(F32) / 1024.0, weight)
    pick = pick.astype(BF16)
    pick_t = pick_t.astype(BF16)

    def select(stage):
        source = (tok, cot)[stage]
        loads[stage].wait()
        chosen = dot(pick, source[...])
        if stage == 1:
            chosen = chosen * weight[:, 0:1]
        for c in range(D // 128):
            tile[c * BLOCK : (c + 1) * BLOCK, :] = chosen[:, c * 128 : (c + 1) * 128]
        for s in range(BLOCK):
            target = merged if s < FLIGHT else give
            f = s % FLIGHT
            value = tile[pl.ds(s, D // 128, stride=BLOCK), :].astype(BF16)
            target[stage, 2 * f] = value[0:16]
            target[stage, 2 * f + 1] = value[16:32]

    def give_pair(stage):
        send(give.at[stage], got.at[stage], pair_s.at[stage], pair_r.at[stage], x_pair)

    def all_z(stage, src, dst, send_sem, recv_sem):
        def body(i, carry):
            step = jnp.where(i % 2 == 1, (i + 1) // 2, Z - i // 2)
            zt = z_at(step)
            remote(src.at[zt], dst.at[z], send_sem, recv_sem, {"expert": zt * X + x}).start()
            return carry

        lax.fori_loop(1, Z, body, 0)
        dst[z] = src[z]
        sent.append(remote(src.at[pl.ds(0, Z - 1)], src.at[pl.ds(0, Z - 1)], send_sem, recv_sem, x_next))

    def merge(stage):
        arrived(got.at[stage], pair_r.at[stage])
        merged[stage] = merged[stage] + got[stage]
        all_z(stage, merged.at[stage], zin.at[stage], z_s.at[stage], z_r.at[stage])

    def place(stage, half, column):
        start = pl.multiple_of((column + X) % X * BLOCK, BLOCK)
        return rows.at[stage, half, pl.ds(start, BLOCK), :]

    def gather(stage):
        arrived(zin.at[stage, pl.ds(0, Z - 1)], z_r.at[stage])
        for i in range(Z):
            tile2[pl.ds(i, 16, stride=Z), :] = zin[stage, i].astype(F32)
        mine = place(stage, h, x)
        for c in range(HALF // 128):
            mine[:, c * 128 : (c + 1) * 128] = tile2[c * BLOCK : (c + 1) * BLOCK, :].astype(BF16)

        def hand(ref, i, to):
            send(ref, ref, ag_s.at[stage, i], ag_r.at[stage, i], to)

        hand(mine, 0, z_pair)
        hand(mine, 1, x_next)
        hand(mine, 2, x_prev)

    def gather_on(stage):
        def hand(ref, i, to):
            send(ref, ref, ag_s.at[stage, i], ag_r.at[stage, i], to)

        def take(ref, i):
            arrived(ref, ag_r.at[stage, i])

        twin = place(stage, 1 - h, x)
        take(twin, 0)
        hand(twin, 3, x_next)
        hand(twin, 4, x_prev)
        left = place(stage, h, x - 1)
        take(left, 1)
        hand(left, 5, x_next)
        right = place(stage, 1 - h, x + 1)
        take(right, 4)
        hand(right, 6, x_prev)
        take(place(stage, h, x + 1), 2)
        take(place(stage, 1 - h, x - 1), 3)
        take(place(stage, h, x + 2), 5)
        take(place(stage, 1 - h, x + 2), 6)

    select(0)
    pl.semaphore_wait(barrier, Z + 4)
    give_pair(0)
    select(1)
    give_pair(1)
    merge(0)
    merge(1)
    gather(0)
    gather(1)
    gather_on(0)
    for copy in loads[2:]:
        copy.wait()
    ab = dot(rows[0, 0], w[0:HALF, :]) + dot(rows[0, 1], w[HALF:D, :])
    gather_on(1)
    dh = lanes(rows[1, 0], wd[:, 0:HALF]) + lanes(rows[1, 1], wd[:, HALF:D])
    a, b = ab[:, 0:HD], ab[:, HD : 2 * HD]
    sig = 1.0 / (1.0 + jnp.exp(-a))
    act = a * sig
    grads = jnp.concatenate(
        (dh * b * sig * (1.0 + a * (1.0 - sig)), dh * act, act * b), axis=1
    )
    dab[...] = grads[:, 0 : 2 * HD].astype(BF16)
    gt[...] = jnp.transpose(grads).astype(BF16)

    def partial(far):
        yt = (y + far) % Y
        half = yt // 4
        cols = pl.ds(pl.multiple_of(yt % 4 * (2 * SLICE), 2 * SLICE), 2 * SLICE)
        gu = dot(gt[0 : 2 * HD, :], rows[0, half, :, cols])
        dn = dot(gt[2 * HD : GRADS, :], rows[1, half, :, cols])
        for c in range(2):
            part[far, c, 0 : 2 * HD, :] = gu[:, c * SLICE : (c + 1) * SLICE].astype(BF16)
            part[far, c, 2 * HD : GRADS, :] = dn[:, c * SLICE : (c + 1) * SLICE].astype(BF16)
        send(part.at[far, 1 - core], d2d.at[far], d2d_s.at[far], d2d_r.at[far], other_core)

    def both_cores(far):
        arrived(d2d.at[far], d2d_r.at[far])

    def own(far, piece):
        lo = piece * PIECE
        return part[far, core, lo : lo + PIECE, :].astype(F32) + d2d[far, lo : lo + PIECE, :].astype(F32)

    def ring(way, hops, piece):
        far = hops if way == 0 else Y - hops
        value = own(far, piece)
        if hops < 3 or (hops == 3 and piece // 2 == way):
            arrived(rin.at[way, hops, piece], ring_r.at[way, hops, piece])
            value = value + rin[way, hops, piece].astype(F32)
        rout[way, hops - 1, piece] = value.astype(BF16)
        send(
            rout.at[way, hops - 1, piece], rin.at[way, hops - 1, piece],
            ring_s.at[way, hops - 1, piece], ring_r.at[way, hops - 1, piece],
            y_next if way == 0 else y_prev,
        )

    def ring_step(hops, late):
        for i in range(2):
            for way in range(2):
                side = way if late else 1 - way
                ring(way, hops, 2 * side + i)

    def p_far():
        lo = pl.multiple_of((1 - h) * HALF, HALF)
        pz_out[...] = lanes(dab[...], w[pl.ds(lo, HALF), :]).astype(BF16)
        send(pz_out, pz_in, pz_sem.at[0], pz_sem.at[1], z_pair)

    def p_near():
        lo = pl.multiple_of(h * HALF, HALF)
        pm[...] = lanes(dab[...], w[pl.ds(lo, HALF), :])

    def p_rows(column, c):
        start = pl.multiple_of((column + X) % X * BLOCK, BLOCK)
        return pm[pl.ds(start, BLOCK), c * MID : (c + 1) * MID]

    def p_a():
        arrived(pz_in, pz_sem.at[1])
        pm[...] = pm[...] + pz_in[...].astype(F32)
        for way in range(2):
            pa_out[way] = p_rows(x + 2, way).astype(BF16)
            send(pa_out.at[way], pa_in.at[way], pa_s.at[way], pa_r.at[way], (x_next, x_prev)[way])
        for way in range(2):
            p_b(way, 1 - way)

    def p_b(way, c):
        value = p_rows(x + 1 if way == 0 else x - 1, c)
        if c == way:
            arrived(pa_in.at[way], pa_r.at[way])
            value = value + pa_in[way].astype(F32)
        pb_out[way, c] = value.astype(BF16)
        send(
            pb_out.at[way, c], pb_in.at[way, c], pb_s.at[way, c], pb_r.at[way, c],
            (x_next, x_prev)[way],
        )

    def p_back():
        for c in range(2):
            value = p_rows(x, c)
            for way in (1 - c, c):
                arrived(pb_in.at[way, c], pb_r.at[way, c])
                value = value + pb_in[way, c].astype(F32)
            for i in range(MID // 128):
                lo = (c * (MID // 128) + i) * BLOCK
                tile2[lo : lo + BLOCK, :] = value[:, i * 128 : (i + 1) * 128]
        for i in range(Z):
            zq_out[i] = tile2[pl.ds(i, 16, stride=Z), :].astype(BF16)
        all_z(0, zq_out, zq_in, zq_sem.at[0], zq_sem.at[1])

    def p_pair():
        arrived(zq_in.at[pl.ds(0, Z - 1)], zq_sem.at[1])
        send(zq_in, pq_in, pq_sem.at[0], pq_sem.at[1], x_pair)

    def p_tokens():
        for f in range(FLIGHT):
            for half in range(2):
                tile[pl.ds(half * 256 + f, 16, stride=BLOCK), :] = zq_in[2 * f + half].astype(F32)
        arrived(pq_in, pq_sem.at[1])
        for f in range(FLIGHT):
            for half in range(2):
                tile[pl.ds(half * 256 + FLIGHT + f, 16, stride=BLOCK), :] = pq_in[2 * f + half].astype(F32)
        for c in range(D // 128):
            prow[:, c * 128 : (c + 1) * 128] = tile[c * BLOCK : (c + 1) * BLOCK, :].astype(BF16)
        tg_out[...] = dot(pick_t, prow[...]).astype(BF16)

    partial(4)
    partial(3)
    partial(5)
    p_far()
    both_cores(4)
    for i in range(2):
        ring(0, 4, i)
        ring(1, 4, 2 + i)
    both_cores(3)
    both_cores(5)
    ring_step(3, False)
    partial(2)
    partial(6)
    ring_step(3, True)
    partial(1)
    partial(7)
    partial(0)
    p_near()
    both_cores(2)
    both_cores(6)
    ring_step(2, False)
    p_a()
    ring_step(2, True)
    for way in range(2):
        p_b(way, way)
    both_cores(1)
    both_cores(7)
    ring_step(1, False)
    p_back()
    ring_step(1, True)
    both_cores(0)
    p_pair()
    p_tokens()

    totals = []
    for piece in range(PIECES):
        value = own(0, piece)
        for way in range(2):
            arrived(rin.at[way, 0, piece], ring_r.at[way, 0, piece])
            value = value + rin[way, 0, piece].astype(F32)
        totals.append(value)
    total = jnp.concatenate(totals, axis=0)
    gg_out[...] = jnp.transpose(total[0:HD]).astype(BF16)
    ug_out[...] = jnp.transpose(total[HD : 2 * HD]).astype(BF16)
    dg_out[...] = total[2 * HD : GRADS].astype(BF16)
    for copy in sent:
        copy.wait_send()


def shards(tokens, cotangent, slot_token, slot_gate, gate_weight, up_weight, down_weight):
    any_space = pl.BlockSpec(memory_space=pl.ANY)
    vmem = pl.BlockSpec(memory_space=pltpu.VMEM)
    smem = pl.BlockSpec(memory_space=pltpu.SMEM)
    dma = pltpu.SemaphoreType.DMA
    return pl.pallas_call(
        kernel,
        out_shape=(
            jax.ShapeDtypeStruct((TOK, D), BF16),
            jax.ShapeDtypeStruct((SLICE, HD), BF16),
            jax.ShapeDtypeStruct((SLICE, HD), BF16),
            jax.ShapeDtypeStruct((HD, SLICE), BF16),
        ),
        in_specs=[smem, smem] + [any_space] * 5,
        out_specs=(vmem,) * 4,
        scratch_shapes=[
            pltpu.VMEM((TOK, D), BF16),
            pltpu.VMEM((TOK, D), BF16),
            pltpu.VMEM((D, 2 * HD), BF16),
            pltpu.VMEM((HD, D), BF16),
            pltpu.VMEM((D // 128 * BLOCK, 128), F32),
            pltpu.VMEM((HALF // 128 * BLOCK, 128), F32),
            pltpu.VMEM((2, Z, 16, 128), BF16),
            pltpu.VMEM((2, Z, 16, 128), BF16),
            pltpu.VMEM((2, Z, 16, 128), BF16),
            pltpu.VMEM((2, Z, 16, 128), BF16),
            pltpu.VMEM((2, 2, ROWS, HALF), BF16),
            pltpu.VMEM((ROWS, 2 * HD), BF16),
            pltpu.VMEM((GRADS, ROWS), BF16),
            pltpu.VMEM((Y, 2, GRADS, SLICE), BF16),
            pltpu.VMEM((Y, GRADS, SLICE), BF16),
            pltpu.VMEM((2, 4, PIECES, PIECE, SLICE), BF16),
            pltpu.VMEM((2, 4, PIECES, PIECE, SLICE), BF16),
            pltpu.VMEM((ROWS, HALF), BF16),
            pltpu.VMEM((ROWS, HALF), BF16),
            pltpu.VMEM((ROWS, HALF), F32),
            pltpu.VMEM((2, BLOCK, MID), BF16),
            pltpu.VMEM((2, BLOCK, MID), BF16),
            pltpu.VMEM((2, 2, BLOCK, MID), BF16),
            pltpu.VMEM((2, 2, BLOCK, MID), BF16),
            pltpu.VMEM((Z, 16, 128), BF16),
            pltpu.VMEM((Z, 16, 128), BF16),
            pltpu.VMEM((Z, 16, 128), BF16),
            pltpu.VMEM((BLOCK, D), BF16),
            dma((5,)),
            dma((2,)),
            dma((2,)),
            dma((2,)),
            dma((2,)),
            dma((2, 7)),
            dma((2, 7)),
            dma((Y,)),
            dma((Y,)),
            dma((2, 4, PIECES)),
            dma((2, 4, PIECES)),
            dma((2,)),
            dma((2,)),
            dma((2,)),
            dma((2, 2)),
            dma((2, 2)),
            dma((2,)),
            dma((2,)),
        ],
        compiler_params=pltpu.CompilerParams(
            collective_id=0, has_side_effects=True, vmem_limit_bytes=40 * 1024 * 1024
        ),
        name="moe_backward",
    )(slot_token, slot_gate, tokens, cotangent, gate_weight, up_weight, down_weight)


def solution(mesh):
    placed = (
        P(("dp", "expert"), None),
        P(("dp", "expert"), None),
        P(("dp", "expert"), None),
        P(("dp", "expert"), None),
        P(None, "expert"),
        P(None, "expert"),
        P("expert", None),
    )
    return jax.shard_map(
        shards,
        mesh=mesh,
        in_specs=placed,
        out_specs=(
            P(("dp", "expert"), None),
            P("dp", "expert"),
            P("dp", "expert"),
            P("expert", "dp"),
        ),
        check_vma=False,
    )
```

time: 358 us -> 92.2 us (0.26)
  the two profiles are of different devices: /device:TPU:1 before, /device:TPU:2 now
where the time goes in v1:
time: 92.2 us; the launch traced here: 91.9 us
  Pallas kernels  80.9 us (88%)
  local copies, waits for them, and re-layouts  10.3 us (11%)
    pallas_call x1, Pallas kernels, shards(): pl.pallas_call(kernel, out_shape=(jax.ShapeDtypeStruct((TOK, D), BF16), j...  80.9 us
    unnamed x18, local copies, waits for them, and re-layouts  10.3 us

profile of v1, /device:TPU:2, one launch (start us, length us, event | category | flops | bytes accessed | tf_op | source)
XLA Modules:
  0.0 91.9 jit_solution(8329054069011907907)
XLA Ops:
  0.6 0.0 copy-start
  0.6 1.2 %copy-done = bf16[128,4096]{1,0:T(8,128)(2,1)S(1)} copy-done((bf16[128,4096]{1,0:T(8,128)(2,1)S(1)}, bf16[128,4096]{1,0:T(8,128)(2,1)}, u32[]{:S(2)}) %copy-start) | copy-done | bytes 1048600
  1.9 0.0 copy-start.1
  1.9 1.2 %copy-done.1 = bf16[128,4096]{1,0:T(8,128)(2,1)S(1)} copy-done((bf16[128,4096]{1,0:T(8,128)(2,1)S(1)}, bf16[128,4096]{1,0:T(8,128)(2,1)}, u32[]{:S(2)}) %copy-start.1) | copy-done | bytes 1048600
  3.1 0.0 copy-start.2
  3.1 1.2 %copy-done.2 = bf16[4096,128]{1,0:T(8,128)(2,1)S(1)} copy-done((bf16[4096,128]{1,0:T(8,128)(2,1)S(1)}, bf16[4096,128]{1,0:T(8,128)(2,1)}, u32[]{:S(2)}) %copy-start.2) | copy-done | bytes 1048600
  4.3 0.0 copy-start.3
  4.3 1.2 %copy-done.3 = bf16[4096,128]{1,0:T(8,128)(2,1)S(1)} copy-done((bf16[4096,128]{1,0:T(8,128)(2,1)S(1)}, bf16[4096,128]{1,0:T(8,128)(2,1)}, u32[]{:S(2)}) %copy-start.3) | copy-done | bytes 1048600
  5.5 0.0 copy-start.4
  5.5 1.2 %copy-done.4 = bf16[128,4096]{1,0:T(8,128)(2,1)S(1)} copy-done((bf16[128,4096]{1,0:T(8,128)(2,1)S(1)}, bf16[128,4096]{1,0:T(8,128)(2,1)}, u32[]{:S(2)}) %copy-start.4) | copy-done | bytes 1048600
  6.8 0.0 copy-start.5
  6.8 0.7 copy-done.5
  7.4 0.0 copy-start.6
  7.4 0.7 copy-done.6
  8.1 80.9 %moe_backward.1 = (bf16[128,4096]{1,0:T(8,128)(2,1)S(1)}, bf16[256,128]{1,0:T(8,128)(2,1)S(1)}, bf16[256,128]{1,0:T(8,128)(2,1)S(1)}, bf16[128,256]{1,0:T(8,128)(2,1)S(1)}) custom-call(s32[1,16]{1,0:T(1,128)S(1)} %copy-done.5, s32[1,16]{1,0:T(1,128)S(1)} %copy-done.6, bf16[128,4096]{1,0:T(8,128)(2,1)S(1)} %copy-done, bf16[128,4096]{1,0:T(8,128)(2,1)S(1)} %copy-done.1, ...), custom_call_target="tpu_custom_call" | custom-call | tf_op jit(solution)/shard_map/moe_backward/pallas_call | solution.py:375
  89.0 1.0 %copy.15 = bf16[128,4096]{1,0:T(8,128)(2,1)} copy(bf16[128,4096]{1,0:T(8,128)(2,1)S(1)} %get-tuple-element.8) | data formatting | bytes 2097152
  90.0 0.6 copy.16
  90.6 0.6 copy.17
  91.2 0.6 copy.18
Async XLA Ops:
  0.6 1.2 %copy-start = (bf16[128,4096]{1,0:T(8,128)(2,1)S(1)}, bf16[128,4096]{1,0:T(8,128)(2,1)}, u32[]{:S(2)}) copy-start(bf16[128,4096]{1,0:T(8,128)(2,1)} %tok_hbm.1) | copy-start | bytes 3145732
  1.9 1.2 %copy-start.1 = (bf16[128,4096]{1,0:T(8,128)(2,1)S(1)}, bf16[128,4096]{1,0:T(8,128)(2,1)}, u32[]{:S(2)}) copy-start(bf16[128,4096]{1,0:T(8,128)(2,1)} %cot_hbm.1) | copy-start | bytes 3145732
  3.1 1.2 %copy-start.2 = (bf16[4096,128]{1,0:T(8,128)(2,1)S(1)}, bf16[4096,128]{1,0:T(8,128)(2,1)}, u32[]{:S(2)}) copy-start(bf16[4096,128]{1,0:T(8,128)(2,1)} %wg_hbm.1) | copy-start | bytes 3145732
  4.3 1.2 %copy-start.3 = (bf16[4096,128]{1,0:T(8,128)(2,1)S(1)}, bf16[4096,128]{1,0:T(8,128)(2,1)}, u32[]{:S(2)}) copy-start(bf16[4096,128]{1,0:T(8,128)(2,1)} %wu_hbm.1) | copy-start | bytes 3145732
  5.5 1.2 %copy-start.4 = (bf16[128,4096]{1,0:T(8,128)(2,1)S(1)}, bf16[128,4096]{1,0:T(8,128)(2,1)}, u32[]{:S(2)}) copy-start(bf16[128,4096]{1,0:T(8,128)(2,1)} %wd_hbm.1) | copy-start | bytes 3145732
  6.8 0.7 copy-start.5
  7.4 0.7 copy-start.6

commit v2 on v1

--- a/solution.py
+++ b/solution.py
@@ -35,13 +35,13 @@
 
 
 def kernel(
-    st, sg, tok_hbm, cot_hbm, wg_hbm, wu_hbm, wd_hbm,
-    tg_out, gg_out, ug_out, dg_out,
-    tok, cot, w, wd, tile, tile2, merged, give, got, zin, rows, dab, gt,
+    st_hbm, sg_hbm, tok_hbm, cot_hbm, wg_hbm, wu_hbm, wd_hbm,
+    prow, pick_out, total_out,
+    st, sg, tok, cot, w, wd, tile, tile2, merged, give, got, zin, rows, dab, gt,
     part, d2d, rout, rin, pz_out, pz_in, pm, pa_out, pa_in, pb_out, pb_in,
-    zq_out, zq_in, pq_in, prow,
+    zq_out, zq_in, pq_in,
     load_sem, pair_s, pair_r, z_s, z_r, ag_s, ag_r, d2d_s, d2d_r, ring_s, ring_r,
-    pz_sem, pa_s, pa_r, pb_s, pb_r, zq_sem, pq_sem,
+    pz_s, pz_r, pa_s, pa_r, pb_s, pb_r, zq_sem, pq_sem,
 ):
     d = lax.axis_index("dp")
     e = lax.axis_index("expert")
@@ -91,6 +91,8 @@
         pltpu.make_async_copy(src, dst, load_sem.at[i])
         for i, (src, dst) in enumerate(
             (
+                (st_hbm, st),
+                (sg_hbm, sg),
                 (tok_hbm, tok),
                 (cot_hbm, cot),
                 (wg_hbm, w.at[:, 0:HD]),
@@ -101,6 +103,9 @@
     ]
     for copy in loads:
         copy.start()
+
+    loads[0].wait()
+    loads[1].wait()
 
     line = lax.broadcasted_iota(jnp.int32, (BLOCK, TOK), 0)
     lane = lax.broadcasted_iota(jnp.int32, (BLOCK, TOK), 1)
@@ -118,11 +123,11 @@
             pick_t = jnp.where((col_t == s) & (row_t == token), 1.0, pick_t)
             weight = jnp.where(line == s, code.astype(F32) / 1024.0, weight)
     pick = pick.astype(BF16)
-    pick_t = pick_t.astype(BF16)
+    pick_out[...] = pick_t.astype(BF16)
 
     def select(stage):
         source = (tok, cot)[stage]
-        loads[stage].wait()
+        loads[2 + stage].wait()
         chosen = dot(pick, source[...])
         if stage == 1:
             chosen = chosen * weight[:, 0:1]
@@ -154,9 +159,15 @@
         merged[stage] = merged[stage] + got[stage]
         all_z(stage, merged.at[stage], zin.at[stage], z_s.at[stage], z_r.at[stage])
 
-    def place(stage, half, column):
+    def place(stage, half, column, lo=0, width=HALF):
         start = pl.multiple_of((column + X) % X * BLOCK, BLOCK)
-        return rows.at[stage, half, pl.ds(start, BLOCK), :]
+        return rows.at[stage, half, pl.ds(start, BLOCK), pl.ds(lo, width)]
+
+    def hand(stage, ref, i, to):
+        send(ref, ref, ag_s.at[stage, i], ag_r.at[stage, i], to)
+
+    def take(stage, ref, i):
+        arrived(ref, ag_r.at[stage, i])
 
     def gather(stage):
         arrived(zin.at[stage, pl.ds(0, Z - 1)], z_r.at[stage])
@@ -165,35 +176,33 @@
         mine = place(stage, h, x)
         for c in range(HALF // 128):
             mine[:, c * 128 : (c + 1) * 128] = tile2[c * BLOCK : (c + 1) * BLOCK, :].astype(BF16)
-
-        def hand(ref, i, to):
-            send(ref, ref, ag_s.at[stage, i], ag_r.at[stage, i], to)
-
-        hand(mine, 0, z_pair)
-        hand(mine, 1, x_next)
-        hand(mine, 2, x_prev)
-
-    def gather_on(stage):
-        def hand(ref, i, to):
-            send(ref, ref, ag_s.at[stage, i], ag_r.at[stage, i], to)
-
-        def take(ref, i):
-            arrived(ref, ag_r.at[stage, i])
-
+        hand(stage, mine, 0, z_pair)
+        hand(stage, mine, 1, x_next)
+        hand(stage, mine, 2, x_prev)
+
+    def gather_far(stage):
+        take(stage, place(stage, h, x - 1), 1)
+        hand(stage, place(stage, h, x - 1, 0, MID), 5, x_next)
+        take(stage, place(stage, h, x + 1), 2)
+        hand(stage, place(stage, h, x + 1, MID, MID), 6, x_prev)
+
+    def gather_twin(stage):
         twin = place(stage, 1 - h, x)
-        take(twin, 0)
-        hand(twin, 3, x_next)
-        hand(twin, 4, x_prev)
-        left = place(stage, h, x - 1)
-        take(left, 1)
-        hand(left, 5, x_next)
-        right = place(stage, 1 - h, x + 1)
-        take(right, 4)
-        hand(right, 6, x_prev)
-        take(place(stage, h, x + 1), 2)
-        take(place(stage, 1 - h, x - 1), 3)
-        take(place(stage, h, x + 2), 5)
-        take(place(stage, 1 - h, x + 2), 6)
+        take(stage, twin, 0)
+        hand(stage, twin, 3, x_next)
+        hand(stage, twin, 4, x_prev)
+
+    def gather_cross(stage):
+        for i in range(2):
+            far = place(stage, h, x + 2, i * MID, MID)
+            take(stage, far, 5 + i)
+            hand(stage, far, 7 + i, z_pair)
+
+    def gather_end(stage):
+        take(stage, place(stage, 1 - h, x - 1), 3)
+        take(stage, place(stage, 1 - h, x + 1), 4)
+        for i in range(2):
+            take(stage, place(stage, 1 - h, x + 2, i * MID, MID), 7 + i)
 
     select(0)
     pl.semaphore_wait(barrier, Z + 4)
@@ -204,11 +213,17 @@
     merge(1)
     gather(0)
     gather(1)
-    gather_on(0)
-    for copy in loads[2:]:
+    gather_far(0)
+    gather_far(1)
+    gather_twin(0)
+    gather_twin(1)
+    gather_cross(0)
+    gather_cross(1)
+    gather_end(0)
+    for copy in loads[4:]:
         copy.wait()
     ab = dot(rows[0, 0], w[0:HALF, :]) + dot(rows[0, 1], w[HALF:D, :])
-    gather_on(1)
+    gather_end(1)
     dh = lanes(rows[1, 0], wd[:, 0:HALF]) + lanes(rows[1, 1], wd[:, HALF:D])
     a, b = ab[:, 0:HD], ab[:, HD : 2 * HD]
     sig = 1.0 / (1.0 + jnp.exp(-a))
@@ -256,42 +271,52 @@
                 side = way if late else 1 - way
                 ring(way, hops, 2 * side + i)
 
+    def p_place(ref, column):
+        start = pl.multiple_of((column + X) % X * BLOCK, BLOCK)
+        return ref.at[pl.ds(start, BLOCK), :]
+
+    p_order = (x + 2, x + 1, x - 1, x)
+
     def p_far():
         lo = pl.multiple_of((1 - h) * HALF, HALF)
         pz_out[...] = lanes(dab[...], w[pl.ds(lo, HALF), :]).astype(BF16)
-        send(pz_out, pz_in, pz_sem.at[0], pz_sem.at[1], z_pair)
+        for i, column in enumerate(p_order):
+            send(
+                p_place(pz_out, column), p_place(pz_in, column), pz_s.at[i], pz_r.at[i], z_pair
+            )
 
     def p_near():
         lo = pl.multiple_of(h * HALF, HALF)
         pm[...] = lanes(dab[...], w[pl.ds(lo, HALF), :])
 
-    def p_rows(column, c):
-        start = pl.multiple_of((column + X) % X * BLOCK, BLOCK)
-        return pm[pl.ds(start, BLOCK), c * MID : (c + 1) * MID]
+    def p_sum(i):
+        arrived(p_place(pz_in, p_order[i]), pz_r.at[i])
+        return p_place(pm, p_order[i])[...] + p_place(pz_in, p_order[i])[...].astype(F32)
 
     def p_a():
-        arrived(pz_in, pz_sem.at[1])
-        pm[...] = pm[...] + pz_in[...].astype(F32)
+        value = p_sum(0)
         for way in range(2):
-            pa_out[way] = p_rows(x + 2, way).astype(BF16)
+            pa_out[way] = value[:, way * MID : (way + 1) * MID].astype(BF16)
             send(pa_out.at[way], pa_in.at[way], pa_s.at[way], pa_r.at[way], (x_next, x_prev)[way])
+
+    def p_b():
         for way in range(2):
-            p_b(way, 1 - way)
-
-    def p_b(way, c):
-        value = p_rows(x + 1 if way == 0 else x - 1, c)
-        if c == way:
-            arrived(pa_in.at[way], pa_r.at[way])
-            value = value + pa_in[way].astype(F32)
-        pb_out[way, c] = value.astype(BF16)
-        send(
-            pb_out.at[way, c], pb_in.at[way, c], pb_s.at[way, c], pb_r.at[way, c],
-            (x_next, x_prev)[way],
-        )
+            value = p_sum(1 + way)
+            for c in (1 - way, way):
+                piece = value[:, c * MID : (c + 1) * MID]
+                if c == way:
+                    arrived(pa_in.at[way], pa_r.at[way])
+                    piece = piece + pa_in[way].astype(F32)
+                pb_out[way, c] = piece.astype(BF16)
+                send(
+                    pb_out.at[way, c], pb_in.at[way, c], pb_s.at[way, c], pb_r.at[way, c],
+                    (x_next, x_prev)[way],
+                )
 
     def p_back():
+        mine = p_sum(3)
         for c in range(2):
-            value = p_rows(x, c)
+            value = mine[:, c * MID : (c + 1) * MID]
             for way in (1 - c, c):
                 arrived(pb_in.at[way, c], pb_r.at[way, c])
                 value = value + pb_in[way, c].astype(F32)
@@ -316,12 +341,11 @@
                 tile[pl.ds(half * 256 + FLIGHT + f, 16, stride=BLOCK), :] = pq_in[2 * f + half].astype(F32)
         for c in range(D // 128):
             prow[:, c * 128 : (c + 1) * 128] = tile[c * BLOCK : (c + 1) * BLOCK, :].astype(BF16)
-        tg_out[...] = dot(pick_t, prow[...]).astype(BF16)
 
     partial(4)
+    p_far()
     partial(3)
     partial(5)
-    p_far()
     both_cores(4)
     for i in range(2):
         ring(0, 4, i)
@@ -329,60 +353,74 @@
     both_cores(3)
     both_cores(5)
     ring_step(3, False)
+    p_near()
     partial(2)
     partial(6)
-    ring_step(3, True)
+    p_a()
     partial(1)
     partial(7)
     partial(0)
-    p_near()
+    ring_step(3, True)
+    p_b()
     both_cores(2)
     both_cores(6)
     ring_step(2, False)
-    p_a()
+    p_back()
     ring_step(2, True)
-    for way in range(2):
-        p_b(way, way)
     both_cores(1)
     both_cores(7)
     ring_step(1, False)
-    p_back()
     ring_step(1, True)
+    p_pair()
     both_cores(0)
-    p_pair()
-    p_tokens()
-
-    totals = []
     for piece in range(PIECES):
         value = own(0, piece)
         for way in range(2):
             arrived(rin.at[way, 0, piece], ring_r.at[way, 0, piece])
             value = value + rin[way, 0, piece].astype(F32)
-        totals.append(value)
-    total = jnp.concatenate(totals, axis=0)
-    gg_out[...] = jnp.transpose(total[0:HD]).astype(BF16)
-    ug_out[...] = jnp.transpose(total[HD : 2 * HD]).astype(BF16)
-    dg_out[...] = total[2 * HD : GRADS].astype(BF16)
+        total_out[piece * PIECE : (piece + 1) * PIECE, :] = value
+    p_tokens()
     for copy in sent:
         copy.wait_send()
 
 
+def finish(prow, pick_t, total, tg_hbm, gg_hbm, ug_hbm, dg_hbm, tg, gg, ug, dg, sems):
+    copies = []
+
+    def out(src, dst):
+        copies.append(pltpu.make_async_copy(src, dst, sems.at[len(copies)]))
+        copies[-1].start()
+
+    for c in range(4):
+        cols = slice(c * (D // 4), (c + 1) * (D // 4))
+        tg[:, cols] = dot(pick_t[...], prow[:, cols]).astype(BF16)
+        out(tg.at[:, cols], tg_hbm.at[:, cols])
+    dg[...] = total[2 * HD : GRADS, :].astype(BF16)
+    out(dg, dg_hbm)
+    gg[...] = jnp.transpose(total[0:HD, :]).astype(BF16)
+    out(gg, gg_hbm)
+    ug[...] = jnp.transpose(total[HD : 2 * HD, :]).astype(BF16)
+    out(ug, ug_hbm)
+    for copy in copies:
+        copy.wait()
+
+
 def shards(tokens, cotangent, slot_token, slot_gate, gate_weight, up_weight, down_weight):
-    any_space = pl.BlockSpec(memory_space=pl.ANY)
+    hbm = pl.BlockSpec(memory_space=pltpu.HBM)
     vmem = pl.BlockSpec(memory_space=pltpu.VMEM)
-    smem = pl.BlockSpec(memory_space=pltpu.SMEM)
     dma = pltpu.SemaphoreType.DMA
-    return pl.pallas_call(
+    prow, pick_t, total = pl.pallas_call(
         kernel,
         out_shape=(
-            jax.ShapeDtypeStruct((TOK, D), BF16),
-            jax.ShapeDtypeStruct((SLICE, HD), BF16),
-            jax.ShapeDtypeStruct((SLICE, HD), BF16),
-            jax.ShapeDtypeStruct((HD, SLICE), BF16),
+            jax.ShapeDtypeStruct((BLOCK, D), BF16),
+            jax.ShapeDtypeStruct((TOK, BLOCK), BF16),
+            jax.ShapeDtypeStruct((GRADS, SLICE), F32),
         ),
-        in_specs=[smem, smem] + [any_space] * 5,
-        out_specs=(vmem,) * 4,
+        in_specs=[hbm] * 7,
+        out_specs=(vmem,) * 3,
         scratch_shapes=[
+            pltpu.SMEM((1, 2 * FLIGHT), jnp.int32),
+            pltpu.SMEM((1, 2 * FLIGHT), jnp.int32),
             pltpu.VMEM((TOK, D), BF16),
             pltpu.VMEM((TOK, D), BF16),
             pltpu.VMEM((D, 2 * HD), BF16),
@@ -410,19 +448,19 @@
             pltpu.VMEM((Z, 16, 128), BF16),
             pltpu.VMEM((Z, 16, 128), BF16),
             pltpu.VMEM((Z, 16, 128), BF16),
-            pltpu.VMEM((BLOCK, D), BF16),
-            dma((5,)),
-            dma((2,)),
-            dma((2,)),
-            dma((2,)),
-            dma((2,)),
-            dma((2, 7)),
-            dma((2, 7)),
+            dma((7,)),
+            dma((2,)),
+            dma((2,)),
+            dma((2,)),
+            dma((2,)),
+            dma((2, 9)),
+            dma((2, 9)),
             dma((Y,)),
             dma((Y,)),
             dma((2, 4, PIECES)),
             dma((2, 4, PIECES)),
-            dma((2,)),
+            dma((4,)),
+            dma((4,)),
             dma((2,)),
             dma((2,)),
             dma((2, 2)),
@@ -431,10 +469,21 @@
             dma((2,)),
         ],
         compiler_params=pltpu.CompilerParams(
-            collective_id=0, has_side_effects=True, vmem_limit_bytes=40 * 1024 * 1024
+            collective_id=0, has_side_effects=True, vmem_limit_bytes=60 * 1024 * 1024
         ),
         name="moe_backward",
     )(slot_token, slot_gate, tokens, cotangent, gate_weight, up_weight, down_weight)
+
+    shapes = ((TOK, D), (SLICE, HD), (SLICE, HD), (HD, SLICE))
+    return pl.pallas_call(
+        finish,
+        out_shape=tuple(jax.ShapeDtypeStruct(shape, BF16) for shape in shapes),
+        in_specs=[vmem] * 3,
+        out_specs=(hbm,) * 4,
+        scratch_shapes=[pltpu.VMEM(shape, BF16) for shape in shapes] + [dma((7,))],
+        compiler_params=pltpu.CompilerParams(vmem_limit_bytes=60 * 1024 * 1024),
+        name="finish",
+    )(prow, pick_t, total)
 
 
 def solution(mesh):

time: 92.2 us -> 73.7 us (0.80)
  local copies, waits for them, and re-layouts: 10.3 us -> 0 us
  Pallas kernels: 80.9 us -> 72.9 us
    unnamed x18 -> x0, local copies, waits for them, and re-layouts: 10.3 us -> none
    pallas_call x1 -> x2, Pallas kernels: 80.9 us -> 72.9 us  [the longest x1 70.5 us: shards(): pl.pallas_call(kernel, out_shape=(jax.ShapeDtypeStruct((BLOCK, D), BF16),...]
where the time goes in v2:
time: 73.7 us; the launch traced here: 73.5 us
  Pallas kernels  72.9 us (99%)
    pallas_call x1, Pallas kernels, shards(): pl.pallas_call(kernel, out_shape=(jax.ShapeDtypeStruct((BLOCK, D), BF16),...  70.5 us
    pallas_call x1, Pallas kernels, shards(): pl.pallas_call(finish, out_shape=tuple((jax.ShapeDtypeStruct(shape, BF16)...  2.36 us

profile of v2, /device:TPU:2, one launch (start us, length us, event | category | flops | bytes accessed | tf_op | source)
XLA Modules:
  0.0 73.5 jit_solution(8483476762827989862)
XLA Ops:
  0.6 70.5 %moe_backward.1 = (bf16[16,4096]{1,0:T(8,128)(2,1)}, bf16[128,16]{1,0:T(8,128)(2,1)}, f32[384,256]{1,0:T(8,128)}) custom-call(s32[1,16]{1,0:T(1,128)} %st_hbm.1, s32[1,16]{1,0:T(1,128)} %sg_hbm.1, bf16[128,4096]{1,0:T(8,128)(2,1)} %tok_hbm.1, bf16[128,4096]{1,0:T(8,128)(2,1)} %cot_hbm.1, bf16[4096,128]{1,0:T(8,128)(2,1)} %wg_hbm.1, ...), custom_call_target="tpu_custom_call" | custom-call | tf_op jit(solution)/shard_map/moe_backward/pallas_call | solution.py:412
  71.1 2.4 %finish.1 = (bf16[128,4096]{1,0:T(8,128)(2,1)}, bf16[256,128]{1,0:T(8,128)(2,1)}, bf16[256,128]{1,0:T(8,128)(2,1)}, bf16[128,256]{1,0:T(8,128)(2,1)}) custom-call(bf16[16,4096]{1,0:T(8,128)(2,1)} %get-tuple-element.7.prow, bf16[128,16]{1,0:T(8,128)(2,1)} %get-tuple-element.8.pick_t, f32[384,256]{1,0:T(8,128)} %get-tuple-element.9.total), custom_call_target="tpu_custom_call" | custom-call | tf_op jit(solution)/shard_map/finish/pallas_call | solution.py:478

commit v3 on v2

--- a/solution.py
+++ b/solution.py
@@ -41,7 +41,7 @@
     part, d2d, rout, rin, pz_out, pz_in, pm, pa_out, pa_in, pb_out, pb_in,
     zq_out, zq_in, pq_in,
     load_sem, pair_s, pair_r, z_s, z_r, ag_s, ag_r, d2d_s, d2d_r, ring_s, ring_r,
-    pz_s, pz_r, pa_s, pa_r, pb_s, pb_r, zq_sem, pq_sem,
+    pz_s, pz_r, pa_s, pa_r, pb_s, pb_r, zq_sem, pq_sem, z_near,
 ):
     d = lax.axis_index("dp")
     e = lax.axis_index("expert")
@@ -77,15 +77,16 @@
     def z_at(i):
         return (z + i) % Z
 
-    def greet(i, carry):
-        pl.semaphore_signal(
-            barrier, inc=1, device_id={"expert": z_at(i) * X + x}, device_id_type=MESH
-        )
-        return carry
-
-    for to in (x_next, x_prev, other_core, y_next, y_prev):
-        pl.semaphore_signal(barrier, inc=1, device_id=to, device_id_type=MESH)
-    lax.fori_loop(1, Z, greet, 0)
+    def z_of(step):
+        return {"expert": z_at(step + Z) * X + x}
+
+    def greet(semaphore, to):
+        pl.semaphore_signal(semaphore, inc=1, device_id=to, device_id_type=MESH)
+
+    near = [z_of(way * step) for step in (4, 3, 2, 1) for way in (1, -1)]
+    near += [x_next, x_prev, other_core, y_next, y_prev]
+    for to in near:
+        greet(barrier, to)
 
     loads = [
         pltpu.make_async_copy(src, dst, load_sem.at[i])
@@ -205,10 +206,13 @@
             take(stage, place(stage, 1 - h, x + 2, i * MID, MID), 7 + i)
 
     select(0)
-    pl.semaphore_wait(barrier, Z + 4)
+    select(1)
+    pl.semaphore_wait(barrier, len(near))
+    for step in (4, -4):
+        greet(z_near, z_of(step))
     give_pair(0)
-    select(1)
     give_pair(1)
+    pl.semaphore_wait(z_near, 2)
     merge(0)
     merge(1)
     gather(0)
@@ -412,9 +416,9 @@
     prow, pick_t, total = pl.pallas_call(
         kernel,
         out_shape=(
-            jax.ShapeDtypeStruct((BLOCK, D), BF16),
-            jax.ShapeDtypeStruct((TOK, BLOCK), BF16),
-            jax.ShapeDtypeStruct((GRADS, SLICE), F32),
+            pltpu.VMEM((BLOCK, D), BF16),
+            pltpu.VMEM((TOK, BLOCK), BF16),
+            pltpu.VMEM((GRADS, SLICE), F32),
         ),
         in_specs=[hbm] * 7,
         out_specs=(vmem,) * 3,
@@ -467,6 +471,7 @@
             dma((2, 2)),
             dma((2,)),
             dma((2,)),
+            pltpu.SemaphoreType.REGULAR,
         ],
         compiler_params=pltpu.CompilerParams(
             collective_id=0, has_side_effects=True, vmem_limit_bytes=60 * 1024 * 1024
@@ -481,7 +486,7 @@
         in_specs=[vmem] * 3,
         out_specs=(hbm,) * 4,
         scratch_shapes=[pltpu.VMEM(shape, BF16) for shape in shapes] + [dma((7,))],
-        compiler_params=pltpu.CompilerParams(vmem_limit_bytes=60 * 1024 * 1024),
+        compiler_params=pltpu.CompilerParams(vmem_limit_bytes=32 * 1024 * 1024),
         name="finish",
     )(prow, pick_t, total)
 

time: 73.7 us -> 70.6 us (0.958)
  Pallas kernels: 72.9 us -> 69.8 us
    pallas_call x1, Pallas kernels: 70.5 us -> 68.5 us  [shards(): pl.pallas_call(kernel, out_shape=(pltpu.VMEM((BLOCK, D), BF16), pltpu.VME...]
    pallas_call x1, Pallas kernels: 2.36 us -> 1.28 us  [shards(): pl.pallas_call(finish, out_shape=tuple((jax.ShapeDtypeStruct(shape, BF16)...]
where the time goes in v3:
time: 70.6 us; the launch traced here: 70.4 us
  Pallas kernels  69.8 us (99%)
    pallas_call x1, Pallas kernels, shards(): pl.pallas_call(kernel, out_shape=(pltpu.VMEM((BLOCK, D), BF16), pltpu.VME...  68.5 us

profile of v3, /device:TPU:2, one launch (start us, length us, event | category | flops | bytes accessed | tf_op | source)
XLA Modules:
  0.0 70.4 jit_solution(6782618823851518004)
XLA Ops:
  0.6 68.5 %moe_backward.1 = (bf16[16,4096]{1,0:T(8,128)(2,1)S(1)}, bf16[128,16]{1,0:T(8,128)(2,1)S(1)}, f32[384,256]{1,0:T(8,128)S(1)}) custom-call(s32[1,16]{1,0:T(1,128)} %st_hbm.1, s32[1,16]{1,0:T(1,128)} %sg_hbm.1, bf16[128,4096]{1,0:T(8,128)(2,1)} %tok_hbm.1, bf16[128,4096]{1,0:T(8,128)(2,1)} %cot_hbm.1, bf16[4096,128]{1,0:T(8,128)(2,1)} %wg_hbm.1, ...), custom_call_target="tpu_custom_call" | custom-call | tf_op jit(solution)/shard_map/moe_backward/pallas_call | solution.py:416
  69.2 1.3 %finish.1 = (bf16[128,4096]{1,0:T(8,128)(2,1)}, bf16[256,128]{1,0:T(8,128)(2,1)}, bf16[256,128]{1,0:T(8,128)(2,1)}, bf16[128,256]{1,0:T(8,128)(2,1)}) custom-call(bf16[16,4096]{1,0:T(8,128)(2,1)S(1)} %get-tuple-element.7.prow, bf16[128,16]{1,0:T(8,128)(2,1)S(1)} %get-tuple-element.8.pick_t, f32[384,256]{1,0:T(8,128)S(1)} %get-tuple-element.9.total), custom_call_target="tpu_custom_call" | custom-call | tf_op jit(solution)/shard_map/finish/pallas_call | solution.py:483

commit v4 on v3

--- a/solution.py
+++ b/solution.py
@@ -56,6 +56,12 @@
     x_pair = {"expert": e + 1 - 2 * (x % 2)}
     z_pair = {"expert": e + X - 2 * X * h}
 
+    places = ((2, 1), (2, 0), (1, 1), (-1, 1), (0, 1), (1, 0), (-1, 0))
+
+    def mate(across, over):
+        column = (x + across + X) % X
+        return {"expert": (z + over * (1 - 2 * h)) * X + column}
+
     def remote(src, dst, send_sem, recv_sem, to):
         return pltpu.make_async_remote_copy(
             src_ref=src, dst_ref=dst, send_sem=send_sem, recv_sem=recv_sem,
@@ -85,6 +91,7 @@
 
     near = [z_of(way * step) for step in (4, 3, 2, 1) for way in (1, -1)]
     near += [x_next, x_prev, other_core, y_next, y_prev]
+    near += [mate(across, over) for across, over in places if across == 2 or over and across]
     for to in near:
         greet(barrier, to)
 
@@ -177,33 +184,12 @@
         mine = place(stage, h, x)
         for c in range(HALF // 128):
             mine[:, c * 128 : (c + 1) * 128] = tile2[c * BLOCK : (c + 1) * BLOCK, :].astype(BF16)
-        hand(stage, mine, 0, z_pair)
-        hand(stage, mine, 1, x_next)
-        hand(stage, mine, 2, x_prev)
-
-    def gather_far(stage):
-        take(stage, place(stage, h, x - 1), 1)
-        hand(stage, place(stage, h, x - 1, 0, MID), 5, x_next)
-        take(stage, place(stage, h, x + 1), 2)
-        hand(stage, place(stage, h, x + 1, MID, MID), 6, x_prev)
-
-    def gather_twin(stage):
-        twin = place(stage, 1 - h, x)
-        take(stage, twin, 0)
-        hand(stage, twin, 3, x_next)
-        hand(stage, twin, 4, x_prev)
-
-    def gather_cross(stage):
-        for i in range(2):
-            far = place(stage, h, x + 2, i * MID, MID)
-            take(stage, far, 5 + i)
-            hand(stage, far, 7 + i, z_pair)
+        for i, (across, over) in enumerate(places):
+            hand(stage, mine, i, mate(across, over))
 
     def gather_end(stage):
-        take(stage, place(stage, 1 - h, x - 1), 3)
-        take(stage, place(stage, 1 - h, x + 1), 4)
-        for i in range(2):
-            take(stage, place(stage, 1 - h, x + 2, i * MID, MID), 7 + i)
+        for i, (across, over) in enumerate(places):
+            take(stage, place(stage, 1 - h if over else h, x - across), i)
 
     select(0)
     select(1)
@@ -217,12 +203,6 @@
     merge(1)
     gather(0)
     gather(1)
-    gather_far(0)
-    gather_far(1)
-    gather_twin(0)
-    gather_twin(1)
-    gather_cross(0)
-    gather_cross(1)
     gather_end(0)
     for copy in loads[4:]:
         copy.wait()
@@ -457,8 +437,8 @@
             dma((2,)),
             dma((2,)),
             dma((2,)),
-            dma((2, 9)),
-            dma((2, 9)),
+            dma((2, 7)),
+            dma((2, 7)),
             dma((Y,)),
             dma((Y,)),
             dma((2, 4, PIECES)),

time: 70.6 us -> 69.3 us (0.982)
  Pallas kernels: 69.8 us -> 68.5 us
    pallas_call x1, Pallas kernels: 68.5 us -> 67.3 us  [shards(): pl.pallas_call(kernel, out_shape=(pltpu.VMEM((BLOCK, D), BF16), pltpu.VME...]
where the time goes in v4:
time: 69.3 us; the launch traced here: 69.2 us
  Pallas kernels  68.5 us (99%)
    pallas_call x1, Pallas kernels, shards(): pl.pallas_call(kernel, out_shape=(pltpu.VMEM((BLOCK, D), BF16), pltpu.VME...  67.3 us

profile of v4, /device:TPU:2, one launch (start us, length us, event | category | flops | bytes accessed | tf_op | source)
XLA Modules:
  0.0 69.2 jit_solution(15177964061196972949)
XLA Ops:
  0.6 67.3 %moe_backward.1 = (bf16[16,4096]{1,0:T(8,128)(2,1)S(1)}, bf16[128,16]{1,0:T(8,128)(2,1)S(1)}, f32[384,256]{1,0:T(8,128)S(1)}) custom-call(s32[1,16]{1,0:T(1,128)} %st_hbm.1, s32[1,16]{1,0:T(1,128)} %sg_hbm.1, bf16[128,4096]{1,0:T(8,128)(2,1)} %tok_hbm.1, bf16[128,4096]{1,0:T(8,128)(2,1)} %cot_hbm.1, bf16[4096,128]{1,0:T(8,128)(2,1)} %wg_hbm.1, ...), custom_call_target="tpu_custom_call" | custom-call | tf_op jit(solution)/shard_map/moe_backward/pallas_call | solution.py:396
  67.9 1.3 %finish.1 = (bf16[128,4096]{1,0:T(8,128)(2,1)}, bf16[256,128]{1,0:T(8,128)(2,1)}, bf16[256,128]{1,0:T(8,128)(2,1)}, bf16[128,256]{1,0:T(8,128)(2,1)}) custom-call(bf16[16,4096]{1,0:T(8,128)(2,1)S(1)} %get-tuple-element.7.prow, bf16[128,16]{1,0:T(8,128)(2,1)S(1)} %get-tuple-element.8.pick_t, f32[384,256]{1,0:T(8,128)S(1)} %get-tuple-element.9.total), custom_call_target="tpu_custom_call" | custom-call | tf_op jit(solution)/shard_map/finish/pallas_call | solution.py:463
